TPU v7x, 32 devices: a whole 2x2x4 slice. The times are simulated.
32 devices in a mesh: shot: 2 (over x), slab: 16 (over z, y, core).
Axes of the slice: x: 2, y: 2, z: 4, core: 2. Of those that a mesh axis runs over, the one named last changes fastest.
Arguments:
- wavefield: float32 [2, 2, 2048, 2048], P('shot', None, 'slab'), parts along dimension 0, may hold values from -5 to 5
- frequencies: float32 [2], P('shot'), parts along dimension 0, may hold values from 1 to 3
- velocity: float32 [1, 2048, 2048], P(None, 'slab'), may hold values from 1 to 2.25, as said below
- bracket: int32 [1, 2048, 2048], P(None, 'slab'), may hold values from 0 to 1
Outputs:
- propagated: float32 [2, 2, 2048, 2048], P('shot', None, 'slab'), parts along dimension 0
- image: float32 [2, 2048, 2048], P('shot', 'slab'), parts along dimension 0
There are 2 independent parts, one for each index of `shot`. A program takes and returns all parts, laid end to end along the dimension named above; an argument that names none is the same for every part. Nothing has to cross between parts.
Inputs may be any that keep to these rules, and one draw needn't show every extreme that they name: velocity[d, y, x] lies between the reference speeds c_b and c_(b+1) with b = bracket[d, x, y].
All inputs are finite; a program needn't handle non-finite values.
Results may differ from a plain program's by a relative error of at most 0.0003.
Values sent between devices are 32-bit elements; how exact they have to be, the bound alone decides.
A program may use at most 64 MiB of HBM per device.

v0:
```python
import math

import jax
import jax.numpy as jnp
import ml_dtypes
import numpy as np
from jax import lax
from jax.experimental import pallas as pl
from jax.experimental.pallas import tpu as pltpu
from jax.sharding import PartitionSpec as P

ref_speeds = (1.0, 1.5, 2.25)
step_length = 1.0
highest = lax.Precision.HIGHEST


def dft_table(height, breadth, modulus, direction):
    down_index = lax.iota(jnp.int32, height)[:, None]
    across_index = lax.iota(jnp.int32, breadth)[None, :]
    angles = (down_index * across_index % modulus).astype(jnp.float32) * (
        direction * 2.0 * math.pi / modulus
    )
    return (jnp.cos(angles), jnp.sin(angles))


def contract(pattern, left_pair, right_pair):

    def product(one_side, other_side):
        return jnp.einsum(pattern, one_side, other_side, precision=highest)

    return (
        product(left_pair[0], right_pair[0]) - product(left_pair[1], right_pair[1]),
        product(left_pair[0], right_pair[1]) + product(left_pair[1], right_pair[0]),
    )


def rotate(values, factor_pair):
    return (
        values[0] * factor_pair[0] - values[1] * factor_pair[1],
        values[0] * factor_pair[1] + values[1] * factor_pair[0],
    )


def forward_lines(fields):
    item_count, row_count, extent = fields[0].shape
    devices = lax.axis_size("slab")
    line_count = extent // devices
    reshaped = tuple(
        (part_now.reshape(item_count, row_count, line_count, devices) for part_now in fields)
    )
    section_one = contract(
        "nrab,ak->nrkb", reshaped, dft_table(line_count, line_count, line_count, -1.0)
    )
    twisted = rotate(
        section_one,
        tuple((turning[None, None] for turning in dft_table(line_count, devices, extent, -1.0))),
    )
    section_two = contract("nrkb,bq->nkqr", twisted, dft_table(devices, devices, devices, -1.0))
    return tuple(
        (part_now.reshape(item_count, line_count, devices * row_count) for part_now in section_two)
    )


def forward_rows(fields):
    item_count, line_count, extent = fields[0].shape
    devices = lax.axis_size("slab")
    row_count = extent // devices
    reshaped = tuple(
        (part_now.reshape(item_count, line_count, devices, row_count) for part_now in fields)
    )
    section_one = contract("ncab,ak->nckb", reshaped, dft_table(devices, devices, devices, -1.0))
    twisted = rotate(
        section_one,
        tuple((turning[None, None] for turning in dft_table(devices, row_count, extent, -1.0))),
    )
    section_two = contract(
        "nckb,bq->nckq", twisted, dft_table(row_count, row_count, row_count, -1.0)
    )
    return tuple((part_now.reshape(item_count, line_count, extent) for part_now in section_two))


def inverse_rows(fields):
    item_count, line_count, extent = fields[0].shape
    devices = lax.axis_size("slab")
    row_count = extent // devices
    reshaped = tuple(
        (part_now.reshape(item_count, line_count, devices, row_count) for part_now in fields)
    )
    section_one = contract(
        "nckq,bq->nckb", reshaped, dft_table(row_count, row_count, row_count, 1.0)
    )
    twisted = rotate(
        section_one,
        tuple((turning[None, None] for turning in dft_table(devices, row_count, extent, 1.0))),
    )
    section_two = contract("nckb,ak->ncab", twisted, dft_table(devices, devices, devices, 1.0))
    return tuple(
        (
            part_now.reshape(item_count, line_count, extent) * (1.0 / extent)
            for part_now in section_two
        )
    )


def inverse_lines(fields):
    item_count, line_count, extent = fields[0].shape
    devices = lax.axis_size("slab")
    row_count = extent // devices
    total_lines = line_count * devices
    reshaped = tuple(
        (part_now.reshape(item_count, line_count, devices, row_count) for part_now in fields)
    )
    section_one = contract("nkqr,bq->nkbr", reshaped, dft_table(devices, devices, devices, 1.0))
    twisted = rotate(
        section_one,
        tuple(
            (
                turning[None, :, :, None]
                for turning in dft_table(line_count, devices, total_lines, 1.0)
            )
        ),
    )
    section_two = contract(
        "nkbr,ak->nrab", twisted, dft_table(line_count, line_count, line_count, 1.0)
    )
    return tuple(
        (
            part_now.reshape(item_count, row_count, total_lines) * (1.0 / total_lines)
            for part_now in section_two
        )
    )


def phase_shift(values, wave_square, angular):
    slowness = 1.0 / jnp.array(ref_speeds, jnp.float32)
    wave_number = angular[:, None] * slowness[None, :]
    vertical = (wave_number * wave_number)[:, :, None, None] - wave_square[None, None]
    root_abs = jnp.sqrt(jnp.abs(vertical))
    real_part = jnp.where(
        vertical >= 0, jnp.cos(step_length * root_abs), jnp.exp(-step_length * root_abs)
    )
    imag_part = jnp.where(vertical >= 0, jnp.sin(step_length * root_abs), 0.0)
    shifted = rotate((values[0][:, None], values[1][:, None]), (real_part, imag_part))
    item_count = values[0].shape[0]
    return tuple(
        (
            part_now.reshape((item_count * len(ref_speeds),) + values[0].shape[1:])
            for part_now in shifted
        )
    )


def weights(speed_grid, chosen):
    speeds = jnp.array(ref_speeds, jnp.float32)
    lower_speed = jnp.zeros_like(speed_grid)
    upper_speed = jnp.zeros_like(speed_grid)
    for ref_index in range(len(ref_speeds) - 1):
        lower_speed = lower_speed + jnp.where(chosen == ref_index, speeds[ref_index], 0.0)
        upper_speed = upper_speed + jnp.where(chosen == ref_index, speeds[ref_index + 1], 0.0)
    fraction = (speed_grid - lower_speed) / (upper_speed - lower_speed)
    residual_phase = 1.0 / speed_grid - ((1.0 - fraction) / lower_speed + fraction / upper_speed)
    coefficients = []
    for ref_index in range(len(ref_speeds)):
        coefficients.append(
            jnp.where(chosen == ref_index, 1.0 - fraction, 0.0)
            + jnp.where(chosen == ref_index - 1, fraction, 0.0)
        )
    return (jnp.stack(coefficients), residual_phase)


def advance(fields, angular, coefficients, residual_phase, spec_square):
    item_count, row_count, extent = fields[0].shape
    prepared = forward_lines(fields)
    spectrum = forward_rows(
        (
            lax.all_to_all(prepared[0], "slab", split_axis=2, concat_axis=2, tiled=True),
            lax.all_to_all(prepared[1], "slab", split_axis=2, concat_axis=2, tiled=True),
        )
    )
    returned = inverse_rows(phase_shift(spectrum, spec_square, angular))
    waves = inverse_lines(
        (
            lax.all_to_all(returned[0], "slab", split_axis=2, concat_axis=2, tiled=True),
            lax.all_to_all(returned[1], "slab", split_axis=2, concat_axis=2, tiled=True),
        )
    )
    ref_count = len(ref_speeds)
    wave_real = waves[0].reshape(item_count, ref_count, row_count, extent)
    wave_imag = waves[1].reshape(item_count, ref_count, row_count, extent)
    blended_real = jnp.sum(coefficients[None] * wave_real, axis=1)
    blended_imag = jnp.sum(coefficients[None] * wave_imag, axis=1)
    angles = angular[:, None, None] * step_length * residual_phase[None]
    return rotate((blended_real, blended_imag), (jnp.cos(angles), jnp.sin(angles)))


def folded(indices, modulus):
    return jnp.minimum(indices, modulus - indices).astype(jnp.float32) * (2.0 * math.pi / modulus)


def per_device(wavefield, frequencies, velocity, bracket):
    devices = lax.axis_size("slab")
    device_index = lax.axis_index("slab")
    row_count = wavefield.shape[2]
    extent_y = wavefield.shape[3]
    extent_x = row_count * devices
    line_count = extent_y // devices
    speed_columns = lax.all_to_all(velocity, "slab", split_axis=2, concat_axis=1, tiled=True)
    speed_rows = jnp.transpose(speed_columns, (0, 2, 1))
    column = lax.iota(jnp.int32, extent_x)
    line_index = lax.iota(jnp.int32, line_count)
    spec_first = folded(column // row_count + devices * (column % row_count), extent_x)
    spec_second = folded(device_index * line_count + line_index, extent_y)
    spec_square = (
        spec_first[None, :] * spec_first[None, :] + spec_second[:, None] * spec_second[:, None]
    )
    current = (wavefield[:, 0], wavefield[:, 1])
    coefficients, residual_phase = weights(speed_rows[0], bracket[0])
    single = (current[0], current[1])
    pieces = [advance(single, frequencies, coefficients, residual_phase, spec_square)]
    current = (
        jnp.concatenate([piece[0] for piece in pieces], axis=0),
        jnp.concatenate([piece[1] for piece in pieces], axis=0),
    )
    image_rows = [jnp.sum(current[0], axis=0)]
    return (jnp.stack(current, axis=1), jnp.stack(image_rows))


lanes = 128
chunk = 8
bfloat = jnp.bfloat16
phase_degree = 9


def split_tables(devices):
    extent = devices * lanes
    block = np.arange(devices)[:, None, None]
    down = np.arange(lanes)[None, :, None]
    across = np.arange(lanes)[None, None, :]
    angles = (down * (block + devices * across) % extent) * (2.0 * math.pi / extent)
    cosine, sine = np.cos(angles), np.sin(angles)
    table = np.concatenate(
        [np.concatenate([cosine, -sine], 2), np.concatenate([sine, cosine], 2)], 1
    ).astype(np.float32)
    pieces = []
    for whole in (table, np.ascontiguousarray(np.swapaxes(table, 1, 2))):
        high = whole.astype(ml_dtypes.bfloat16)
        pieces += [high, (whole - high.astype(np.float32)).astype(ml_dtypes.bfloat16)]
    return pieces


def phase_series():
    top = 9.1
    nodes = 0.5 * top * (1.0 + np.cos(math.pi * (np.arange(64) + 0.5) / 64))
    root = np.sqrt(nodes)
    out = []
    for values in (np.cos(root), np.sin(root) / root):
        fit = np.polynomial.chebyshev.Chebyshev.fit(nodes, values, phase_degree, domain=[0, top])
        out.append([float(c) for c in fit.convert(kind=np.polynomial.Polynomial).coef])
    return out


def horner(coefficients, u):
    total = jnp.full_like(u, coefficients[-1])
    for c in coefficients[-2::-1]:
        total = total * u + c
    return total


def halves(values):
    high = values.astype(bfloat)
    return high, (values - high.astype(jnp.float32)).astype(bfloat)


def dot(left, right):
    return jnp.dot(left, right, preferred_element_type=jnp.float32)


def dot_right(values, high, low):
    top, rest = halves(values)
    return dot(top, high) + (dot(rest, high) + dot(top, low))


def dot_left(high, low, values):
    top, rest = halves(values)
    return dot(high, top) + (dot(high, rest) + dot(low, top))


def butterflies(values, sign):
    count = len(values)
    if count == 1:
        return values
    even = butterflies(values[0::2], sign)
    odd = butterflies(values[1::2], sign)
    half = count // 2
    first, second = [], []
    for k in range(half):
        re, im = odd[k]
        if k == 0:
            pass
        elif 4 * k == count:
            re, im = -sign * im, sign * re
        elif 8 * k == count:
            h = math.sqrt(0.5)
            re, im = h * (re - sign * im), h * (im + sign * re)
        elif 8 * k == 3 * count:
            h = math.sqrt(0.5)
            re, im = -h * (re + sign * im), h * (sign * re - im)
        else:
            c = math.cos(2.0 * math.pi * k / count)
            s = sign * math.sin(2.0 * math.pi * k / count)
            re, im = c * re - s * im, c * im + s * re
        er, ei = even[k]
        first.append((er + re, ei + im))
        second.append((er - re, ei - im))
    return first + second


def migrate_kernel(
    devices,
    wave_ref, freq_ref, vel_ref, bracket_ref, ah_ref, al_ref, th_ref, tl_ref,
    out_ref, image_ref,
    lines, sends, spec, factors, parts, waves, speed_recv, coef, turn,
    send_f, recv_f, send_v, recv_v, send_p, recv_p,
):
    me = lax.axis_index("slab")
    refs = len(ref_speeds)
    steps = lanes // chunk
    extent = devices * lanes
    cos_series, sin_series = phase_series()

    def forward_copy(target, block):
        return pltpu.make_async_remote_copy(
            src_ref=sends.at[target], dst_ref=spec.at[block],
            send_sem=send_f.at[target], recv_sem=recv_f.at[block],
            device_id={"slab": target}, device_id_type=pl.DeviceIdType.MESH,
        )

    def speed_copy(target, block):
        return pltpu.make_async_remote_copy(
            src_ref=vel_ref.at[0, :, pl.ds(pl.multiple_of(target * lanes, lanes), lanes)],
            dst_ref=speed_recv.at[block],
            send_sem=send_v.at[target], recv_sem=recv_v.at[block],
            device_id={"slab": target}, device_id_type=pl.DeviceIdType.MESH,
        )

    def part_copy(j, target, block):
        return pltpu.make_async_remote_copy(
            src_ref=parts.at[j, target], dst_ref=waves.at[j, block],
            send_sem=send_p.at[j, target], recv_sem=recv_p.at[j, block],
            device_id={"slab": target}, device_id_type=pl.DeviceIdType.MESH,
        )

    def peer(step):
        return lax.rem(me + step, devices)

    def origin(step):
        return lax.rem(me + devices - step, devices)

    barrier = pltpu.get_barrier_semaphore()

    @pl.loop(1, devices)
    def _(step):
        pl.semaphore_signal(
            barrier, inc=1, device_id={"slab": peer(step)}, device_id_type=pl.DeviceIdType.MESH
        )

    @pl.loop(0, steps)
    def _(i):
        rows = pl.ds(pl.multiple_of(i * chunk, chunk), chunk)
        values = [
            (
                wave_ref[0, 0, rows, a * lanes : (a + 1) * lanes],
                wave_ref[0, 1, rows, a * lanes : (a + 1) * lanes],
            )
            for a in range(devices)
        ]
        for k, (re, im) in enumerate(butterflies(values, -1.0)):
            lines[k, rows, :lanes] = re
            lines[k, rows, lanes:] = im

    pl.semaphore_wait(barrier, devices - 1)

    @pl.loop(1, devices)
    def _(step):
        k = peer(step)
        got = dot_right(lines[k], ah_ref[k], al_ref[k])
        sends[k, :lanes, :] = got[:, :lanes]
        sends[k, lanes:, :] = got[:, lanes:]
        forward_copy(k, me).start()

    got = dot_right(lines[me], ah_ref[me], al_ref[me])
    spec[me, :lanes, :] = got[:, :lanes]
    spec[me, lanes:, :] = got[:, lanes:]

    @pl.loop(1, devices)
    def _(step):
        speed_copy(peer(step), me).start()

    angular = freq_ref[0]
    unit = 2.0 * math.pi / extent
    tall = 4 * chunk
    line_index = me + devices * lax.broadcasted_iota(jnp.int32, (tall, lanes), 1)
    second = jnp.minimum(line_index, extent - line_index).astype(jnp.float32) * unit
    second_square = second * second
    row_iota = lax.broadcasted_iota(jnp.int32, (tall, lanes), 0)
    scale = 1.0 / (extent * extent)

    @pl.loop(0, devices)
    def _(k):
        @pl.loop(0, lanes // tall)
        def _(i):
            start = pl.multiple_of(i * tall, tall)
            column = k + devices * (row_iota + start)
            first = jnp.minimum(column, extent - column).astype(jnp.float32) * unit
            square = first * first + second_square
            for j, speed in enumerate(ref_speeds):
                number = angular * np.float32(1.0 / speed)
                vertical = number * number - square
                root = jnp.sqrt(jnp.abs(vertical))
                decayed = jnp.exp(-root)
                real = jnp.where(vertical >= 0, horner(cos_series, vertical), decayed)
                imag = jnp.where(vertical >= 0, root * horner(sin_series, vertical), 0.0)
                factors[j, k, pl.ds(start, tall), :] = real * scale
                factors[j, k, pl.ds(start + lanes, tall), :] = imag * scale

    @pl.loop(1, devices)
    def _(step):
        k = origin(step)
        forward_copy(k, k).wait_recv()

    def across(ref, sign):
        @pl.loop(0, steps)
        def _(i):
            top = pl.ds(pl.multiple_of(i * chunk, chunk), chunk)
            low = pl.ds(pl.multiple_of(i * chunk + lanes, chunk), chunk)
            values = [(ref[d, top, :], ref[d, low, :]) for d in range(devices)]
            for k, (re, im) in enumerate(butterflies(values, sign)):
                ref[k, top, :] = re
                ref[k, low, :] = im

    across(spec, -1.0)

    for j in range(refs):

        @pl.loop(0, devices)
        def _(k):
            if j == 0:
                spec[k] = dot_left(th_ref[k], tl_ref[k], spec[k])
            re, im = spec[k, :lanes, :], spec[k, lanes:, :]
            fr, fi = factors[j, k, :lanes, :], factors[j, k, lanes:, :]
            shifted = jnp.concatenate([re * fr - im * fi, re * fi + im * fr], axis=0)
            parts[j, k] = dot_left(ah_ref[k], al_ref[k], shifted)

        across(parts.at[j], 1.0)

        @pl.loop(1, devices)
        def _(step):
            part_copy(j, peer(step), me).start()

        waves[j, me] = parts[j, me]

    speed_recv[me] = vel_ref[0, :, pl.ds(pl.multiple_of(me * lanes, lanes), lanes)]

    @pl.loop(1, devices)
    def _(step):
        k = origin(step)
        speed_copy(k, k).wait_recv()

    for a in range(devices):
        cols = slice(a * lanes, (a + 1) * lanes)
        speed = speed_recv[a].T
        chosen = bracket_ref[0, :, cols]
        is_low = chosen == 0
        lower = jnp.where(is_low, ref_speeds[0], ref_speeds[1])
        upper = jnp.where(is_low, ref_speeds[1], ref_speeds[2])
        fraction = (speed - lower) / (upper - lower)
        residual = 1.0 / speed - ((1.0 - fraction) / lower + fraction / upper)
        rest = 1.0 - fraction
        coef[0, :, cols] = jnp.where(is_low, rest, 0.0)
        coef[1, :, cols] = jnp.where(is_low, fraction, rest)
        coef[2, :, cols] = jnp.where(is_low, 0.0, fraction)
        angle = angular * step_length * residual
        u = angle * angle
        turn[0, :, cols] = horner([1.0, -1 / 2, 1 / 24, -1 / 720, 1 / 40320], u)
        turn[1, :, cols] = angle * horner([1.0, -1 / 6, 1 / 120, -1 / 5040], u)

    for j in range(refs):

        @pl.loop(0, devices)
        def _(step):
            k = origin(step)

            @pl.when(step > 0)
            def _():
                part_copy(j, k, k).wait_recv()

            row = jnp.concatenate([waves[j, k, :lanes, :], waves[j, k, lanes:, :]], axis=1)
            got = dot_right(row, th_ref[k], tl_ref[k])
            waves[j, k, :lanes, :] = got[:, :lanes]
            waves[j, k, lanes:, :] = got[:, lanes:]

        @pl.loop(0, steps)
        def _(i):
            top = pl.ds(pl.multiple_of(i * chunk, chunk), chunk)
            low = pl.ds(pl.multiple_of(i * chunk + lanes, chunk), chunk)
            values = [(waves[j, k, top, :], waves[j, k, low, :]) for k in range(devices)]
            for a, (re, im) in enumerate(butterflies(values, 1.0)):
                cols = slice(a * lanes, (a + 1) * lanes)
                weight = coef[j, top, cols]
                re, im = re * weight, im * weight
                if j > 0:
                    re = re + out_ref[0, 0, top, cols]
                    im = im + out_ref[0, 1, top, cols]
                if j == refs - 1:
                    c, s = turn[0, top, cols], turn[1, top, cols]
                    re, im = re * c - im * s, re * s + im * c
                    image_ref[0, top, cols] = re
                out_ref[0, 0, top, cols] = re
                out_ref[0, 1, top, cols] = im

    @pl.loop(1, devices)
    def _(step):
        k = peer(step)
        forward_copy(k, me).wait_send()
        speed_copy(k, me).wait_send()
        for j in range(refs):
            part_copy(j, k, me).wait_send()


def migrate(devices, wavefield, frequencies, velocity, bracket):
    refs = len(ref_speeds)
    tables = [jnp.asarray(piece) for piece in split_tables(devices)]
    extent = devices * lanes
    vmem = pl.BlockSpec(memory_space=pltpu.VMEM)
    tall = 2 * lanes
    single = jnp.float32
    return pl.pallas_call(
        lambda *args: migrate_kernel(devices, *args),
        out_shape=(
            jax.ShapeDtypeStruct((1, 2, lanes, extent), single),
            jax.ShapeDtypeStruct((1, lanes, extent), single),
        ),
        in_specs=[vmem, pl.BlockSpec(memory_space=pltpu.SMEM)] + [vmem] * 6,
        out_specs=(vmem, vmem),
        scratch_shapes=[
            pltpu.VMEM((devices, lanes, tall), single),
            pltpu.VMEM((devices, tall, lanes), single),
            pltpu.VMEM((devices, tall, lanes), single),
            pltpu.VMEM((refs, devices, tall, lanes), single),
            pltpu.VMEM((refs, devices, tall, lanes), single),
            pltpu.VMEM((refs, devices, tall, lanes), single),
            pltpu.VMEM((devices, lanes, lanes), single),
            pltpu.VMEM((refs, lanes, extent), single),
            pltpu.VMEM((2, lanes, extent), single),
            pltpu.SemaphoreType.DMA((devices,)),
            pltpu.SemaphoreType.DMA((devices,)),
            pltpu.SemaphoreType.DMA((devices,)),
            pltpu.SemaphoreType.DMA((devices,)),
            pltpu.SemaphoreType.DMA((refs, devices)),
            pltpu.SemaphoreType.DMA((refs, devices)),
        ],
        compiler_params=pltpu.CompilerParams(
            collective_id=0, has_side_effects=True, vmem_limit_bytes=60 * 2**20
        ),
    )(wavefield, frequencies, velocity, bracket, *tables)


def on_device(wavefield, frequencies, velocity, bracket):
    devices = lax.axis_size("slab")
    fits = (
        wavefield.shape[0] == 1
        and velocity.shape[0] == 1
        and wavefield.shape[2] == lanes
        and wavefield.shape[3] == devices * lanes
        and devices in (2, 4, 8, 16)
    )
    if fits:
        return migrate(devices, wavefield, frequencies, velocity, bracket)
    return per_device(wavefield, frequencies, velocity, bracket)


def solution(mesh):
    return jax.shard_map(
        on_device,
        mesh=mesh,
        in_specs=(
            P("shot", None, "slab", None),
            P("shot"),
            P(None, "slab", None),
            P(None, "slab", None),
        ),
        out_specs=(P("shot", None, "slab", None), P("shot", "slab", None)),
        check_vma=False,
    )
```

profile of v0, /device:TPU:29, one launch (start us, length us, event | category | flops | bytes accessed | tf_op | source)
XLA Modules:
  0.0 229.6 jit_solution(12941465185454108121)
XLA Ops:
  1.3 224.2 %shard_map.95 = (f32[1,2,128,2048]{3,2,1,0:T(8,128)}, f32[1,128,2048]{2,1,0:T(8,128)}) custom-call(f32[1,2,128,2048]{3,2,1,0:T(8,128)} %args_0_.4, f32[1]{0:T(128)S(6)} %copy.12.args_1_, f32[1,128,2048]{2,1,0:T(8,128)} %args_2_.4, s32[1,128,2048]{2,1,0:T(8,128)} %args_3_.4, bf16[16,256,256]{2,1,0:T(8,128)(2,1)} %constant.8.clone.args_4_, ...), custom_call_target="tpu_custom_call" | custom-call | tf_op jit(solution)/shard_map/pallas_call | solution.py:537
  225.4 0.0 copy-start
  225.4 3.2 %copy.13 = f32[1,2,128,2048]{3,2,1,0:T(8,128)} copy(f32[1,2,128,2048]{3,2,1,0:T(8,128)} %get-tuple-element.4) | data formatting | bytes 4194304
  228.7 0.0 copy-done
  228.7 1.0 copy.14
Async XLA Ops:
  225.4 3.2 %copy-start = (f32[1,128,2048]{2,1,0:T(8,128)S(1)}, f32[1,128,2048]{2,1,0:T(8,128)}, u32[]{:S(2)}) copy-start(f32[1,128,2048]{2,1,0:T(8,128)} %get-tuple-element.5) | copy-start | bytes 3145732
where the time goes:
time: 230 us
  Pallas kernels  224 us (97%)
  local copies, waits for them, and re-layouts  4.2 us (2%)
    pallas_call x1, Pallas kernels, migrate(): pl.pallas_call(lambda *args: migrate_kernel(devices, *args), out_shape=(j...  224 us

commit v1 on v0

--- a/solution.py
+++ b/solution.py
@@ -285,41 +285,54 @@
     return dot(high, top) + (dot(high, rest) + dot(low, top))
 
 
+def turned(value, k, count, sign):
+    re, im = value
+    h = math.sqrt(0.5)
+    if k == 0:
+        return re, im
+    if 4 * k == count:
+        return -sign * im, sign * re
+    if 8 * k == count:
+        return h * (re - sign * im), h * (im + sign * re)
+    if 8 * k == 3 * count:
+        return -h * (re + sign * im), h * (sign * re - im)
+    c = math.cos(2.0 * math.pi * k / count)
+    s = sign * math.sin(2.0 * math.pi * k / count)
+    return c * re - s * im, c * im + s * re
+
+
 def butterflies(values, sign):
     count = len(values)
     if count == 1:
         return values
     even = butterflies(values[0::2], sign)
     odd = butterflies(values[1::2], sign)
-    half = count // 2
     first, second = [], []
-    for k in range(half):
-        re, im = odd[k]
-        if k == 0:
-            pass
-        elif 4 * k == count:
-            re, im = -sign * im, sign * re
-        elif 8 * k == count:
-            h = math.sqrt(0.5)
-            re, im = h * (re - sign * im), h * (im + sign * re)
-        elif 8 * k == 3 * count:
-            h = math.sqrt(0.5)
-            re, im = -h * (re + sign * im), h * (sign * re - im)
-        else:
-            c = math.cos(2.0 * math.pi * k / count)
-            s = sign * math.sin(2.0 * math.pi * k / count)
-            re, im = c * re - s * im, c * im + s * re
+    for k in range(count // 2):
         er, ei = even[k]
+        re, im = turned(odd[k], k, count, sign)
         first.append((er + re, ei + im))
         second.append((er - re, ei - im))
     return first + second
+
+
+def half_butterflies(values, sign, side):
+    count = len(values)
+    even = butterflies(values[0::2], sign)
+    odd = butterflies(values[1::2], sign)
+    out = []
+    for k in range(count // 2):
+        er, ei = even[k]
+        re, im = turned(odd[k], k, count, sign)
+        out.append((er + side * re, ei + side * im))
+    return out
 
 
 def migrate_kernel(
     devices,
     wave_ref, freq_ref, vel_ref, bracket_ref, ah_ref, al_ref, th_ref, tl_ref,
     out_ref, image_ref,
-    lines, sends, spec, factors, parts, waves, speed_recv, coef, turn,
+    lines, sends, spec, factors, mixed, parts, waves, speed_recv, coef, turn,
     send_f, recv_f, send_v, recv_v, send_p, recv_p,
 ):
     me = lax.axis_index("slab")
@@ -328,10 +341,15 @@
     extent = devices * lanes
     cos_series, sin_series = phase_series()
 
-    def forward_copy(target, block):
+    half = devices // 2
+    place = lax.rem(me, half)
+    base = me - place
+    other = half - base
+
+    def forward_copy(e, target, block):
         return pltpu.make_async_remote_copy(
-            src_ref=sends.at[target], dst_ref=spec.at[block],
-            send_sem=send_f.at[target], recv_sem=recv_f.at[block],
+            src_ref=sends.at[e * half + lax.rem(target, half)], dst_ref=spec.at[e, block],
+            send_sem=send_f.at[e, target], recv_sem=recv_f.at[e, block],
             device_id={"slab": target}, device_id_type=pl.DeviceIdType.MESH,
         )
 
@@ -343,12 +361,18 @@
             device_id={"slab": target}, device_id_type=pl.DeviceIdType.MESH,
         )
 
-    def part_copy(j, target, block):
+    def part_copy(j, e, target, block):
         return pltpu.make_async_remote_copy(
-            src_ref=parts.at[j, target], dst_ref=waves.at[j, block],
-            send_sem=send_p.at[j, target], recv_sem=recv_p.at[j, block],
-            device_id={"slab": target}, device_id_type=pl.DeviceIdType.MESH,
-        )
+            src_ref=parts.at[j, e, target], dst_ref=waves.at[j, e * half + block],
+            send_sem=send_p.at[j, e, target], recv_sem=recv_p.at[j, e, block],
+            device_id={"slab": base + target}, device_id_type=pl.DeviceIdType.MESH,
+        )
+
+    def near(step):
+        return lax.rem(place + step, half)
+
+    def near_origin(step):
+        return lax.rem(place + half - step, half)
 
     def peer(step):
         return lax.rem(me + step, devices)
@@ -380,17 +404,22 @@
 
     pl.semaphore_wait(barrier, devices - 1)
 
-    @pl.loop(1, devices)
-    def _(step):
-        k = peer(step)
-        got = dot_right(lines[k], ah_ref[k], al_ref[k])
-        sends[k, :lanes, :] = got[:, :lanes]
-        sends[k, lanes:, :] = got[:, lanes:]
-        forward_copy(k, me).start()
-
-    got = dot_right(lines[me], ah_ref[me], al_ref[me])
-    spec[me, :lanes, :] = got[:, :lanes]
-    spec[me, lanes:, :] = got[:, lanes:]
+    for e in range(2):
+
+        @pl.loop(0, half)
+        def _(step):
+            k = near(step)
+            c = e * half + k
+            got = dot_right(lines[c], ah_ref[c], al_ref[c])
+            sends[c, :lanes, :] = got[:, :lanes]
+            sends[c, lanes:, :] = got[:, lanes:]
+            forward_copy(e, other + k, me).start()
+
+            @pl.when(step > 0)
+            def _():
+                forward_copy(e, base + k, me).start()
+
+        spec[e, me] = sends[e * half + place]
 
     @pl.loop(1, devices)
     def _(step):
@@ -399,65 +428,76 @@
     angular = freq_ref[0]
     unit = 2.0 * math.pi / extent
     tall = 4 * chunk
-    line_index = me + devices * lax.broadcasted_iota(jnp.int32, (tall, lanes), 1)
-    second = jnp.minimum(line_index, extent - line_index).astype(jnp.float32) * unit
-    second_square = second * second
     row_iota = lax.broadcasted_iota(jnp.int32, (tall, lanes), 0)
+    lane_iota = lax.broadcasted_iota(jnp.int32, (tall, lanes), 1)
     scale = 1.0 / (extent * extent)
-
-    @pl.loop(0, devices)
-    def _(k):
-        @pl.loop(0, lanes // tall)
-        def _(i):
-            start = pl.multiple_of(i * tall, tall)
-            column = k + devices * (row_iota + start)
-            first = jnp.minimum(column, extent - column).astype(jnp.float32) * unit
-            square = first * first + second_square
-            for j, speed in enumerate(ref_speeds):
-                number = angular * np.float32(1.0 / speed)
-                vertical = number * number - square
-                root = jnp.sqrt(jnp.abs(vertical))
-                decayed = jnp.exp(-root)
-                real = jnp.where(vertical >= 0, horner(cos_series, vertical), decayed)
-                imag = jnp.where(vertical >= 0, root * horner(sin_series, vertical), 0.0)
-                factors[j, k, pl.ds(start, tall), :] = real * scale
-                factors[j, k, pl.ds(start + lanes, tall), :] = imag * scale
-
-    @pl.loop(1, devices)
-    def _(step):
-        k = origin(step)
-        forward_copy(k, k).wait_recv()
-
-    def across(ref, sign):
+    side = (1 - 2 * (base // half)).astype(jnp.float32)
+
+    def make_factors(e):
+        line_index = e * half + place + devices * lane_iota
+        second = jnp.minimum(line_index, extent - line_index).astype(jnp.float32) * unit
+        second_square = second * second
+
+        @pl.loop(0, devices)
+        def _(k):
+            @pl.loop(0, lanes // tall)
+            def _(i):
+                start = pl.multiple_of(i * tall, tall)
+                column = k + devices * (row_iota + start)
+                first = jnp.minimum(column, extent - column).astype(jnp.float32) * unit
+                square = first * first + second_square
+                for j, speed in enumerate(ref_speeds):
+                    number = angular * np.float32(1.0 / speed)
+                    vertical = number * number - square
+                    root = jnp.sqrt(jnp.abs(vertical))
+                    decayed = jnp.exp(-root)
+                    real = jnp.where(vertical >= 0, horner(cos_series, vertical), decayed)
+                    imag = jnp.where(vertical >= 0, root * horner(sin_series, vertical), 0.0)
+                    factors[j, k, pl.ds(start, tall), :] = real * scale
+                    factors[j, k, pl.ds(start + lanes, tall), :] = imag * scale
+
+    def across(ref, out, transform):
         @pl.loop(0, steps)
         def _(i):
             top = pl.ds(pl.multiple_of(i * chunk, chunk), chunk)
             low = pl.ds(pl.multiple_of(i * chunk + lanes, chunk), chunk)
             values = [(ref[d, top, :], ref[d, low, :]) for d in range(devices)]
-            for k, (re, im) in enumerate(butterflies(values, sign)):
-                ref[k, top, :] = re
-                ref[k, low, :] = im
-
-    across(spec, -1.0)
-
-    for j in range(refs):
-
-        @pl.loop(0, devices)
-        def _(k):
-            if j == 0:
-                spec[k] = dot_left(th_ref[k], tl_ref[k], spec[k])
-            re, im = spec[k, :lanes, :], spec[k, lanes:, :]
-            fr, fi = factors[j, k, :lanes, :], factors[j, k, lanes:, :]
-            shifted = jnp.concatenate([re * fr - im * fi, re * fi + im * fr], axis=0)
-            parts[j, k] = dot_left(ah_ref[k], al_ref[k], shifted)
-
-        across(parts.at[j], 1.0)
-
-        @pl.loop(1, devices)
+            for k, (re, im) in enumerate(transform(values)):
+                out[k, top, :] = re
+                out[k, low, :] = im
+
+    for e in range(2):
+        make_factors(e)
+
+        @pl.loop(0, half)
         def _(step):
-            part_copy(j, peer(step), me).start()
-
-        waves[j, me] = parts[j, me]
+            k = near_origin(step)
+            forward_copy(e, other + k, other + k).wait_recv()
+
+            @pl.when(step > 0)
+            def _():
+                forward_copy(e, base + k, base + k).wait_recv()
+
+        across(spec.at[e], spec.at[e], lambda values: butterflies(values, -1.0))
+
+        for j in range(refs):
+
+            @pl.loop(0, devices)
+            def _(k):
+                if j == 0:
+                    spec[e, k] = dot_left(th_ref[k], tl_ref[k], spec[e, k])
+                re, im = spec[e, k, :lanes, :], spec[e, k, lanes:, :]
+                fr, fi = factors[j, k, :lanes, :], factors[j, k, lanes:, :]
+                shifted = jnp.concatenate([re * fr - im * fi, re * fi + im * fr], axis=0)
+                mixed[k] = dot_left(ah_ref[k], al_ref[k], shifted)
+
+            across(mixed, parts.at[j, e], lambda values: half_butterflies(values, 1.0, side))
+
+            @pl.loop(1, half)
+            def _(step):
+                part_copy(j, e, near(step), place).start()
+
+            waves[j, e * half + place] = parts[j, e, place]
 
     speed_recv[me] = vel_ref[0, :, pl.ds(pl.multiple_of(me * lanes, lanes), lanes)]
 
@@ -484,20 +524,26 @@
         turn[0, :, cols] = horner([1.0, -1 / 2, 1 / 24, -1 / 720, 1 / 40320], u)
         turn[1, :, cols] = angle * horner([1.0, -1 / 6, 1 / 120, -1 / 5040], u)
 
-    for j in range(refs):
-
-        @pl.loop(0, devices)
+    def receive(j, e):
+        @pl.loop(0, half)
         def _(step):
-            k = origin(step)
+            block = near_origin(step)
+            k = e * half + block
 
             @pl.when(step > 0)
             def _():
-                part_copy(j, k, k).wait_recv()
+                part_copy(j, e, block, block).wait_recv()
 
             row = jnp.concatenate([waves[j, k, :lanes, :], waves[j, k, lanes:, :]], axis=1)
             got = dot_right(row, th_ref[k], tl_ref[k])
             waves[j, k, :lanes, :] = got[:, :lanes]
             waves[j, k, lanes:, :] = got[:, lanes:]
+
+    for j in range(refs):
+        receive(j, 0)
+
+    for j in range(refs):
+        receive(j, 1)
 
         @pl.loop(0, steps)
         def _(i):
@@ -520,11 +566,20 @@
 
     @pl.loop(1, devices)
     def _(step):
-        k = peer(step)
-        forward_copy(k, me).wait_send()
-        speed_copy(k, me).wait_send()
-        for j in range(refs):
-            part_copy(j, k, me).wait_send()
+        speed_copy(peer(step), me).wait_send()
+
+    for e in range(2):
+
+        @pl.loop(0, half)
+        def _(step):
+            k = near(step)
+            forward_copy(e, other + k, me).wait_send()
+
+            @pl.when(step > 0)
+            def _():
+                forward_copy(e, base + k, me).wait_send()
+                for j in range(refs):
+                    part_copy(j, e, k, place).wait_send()
 
 
 def migrate(devices, wavefield, frequencies, velocity, bracket):
@@ -532,6 +587,7 @@
     tables = [jnp.asarray(piece) for piece in split_tables(devices)]
     extent = devices * lanes
     vmem = pl.BlockSpec(memory_space=pltpu.VMEM)
+    half = devices // 2
     tall = 2 * lanes
     single = jnp.float32
     return pl.pallas_call(
@@ -545,19 +601,20 @@
         scratch_shapes=[
             pltpu.VMEM((devices, lanes, tall), single),
             pltpu.VMEM((devices, tall, lanes), single),
+            pltpu.VMEM((2, devices, tall, lanes), single),
+            pltpu.VMEM((refs, devices, tall, lanes), single),
             pltpu.VMEM((devices, tall, lanes), single),
-            pltpu.VMEM((refs, devices, tall, lanes), single),
-            pltpu.VMEM((refs, devices, tall, lanes), single),
+            pltpu.VMEM((refs, 2, half, tall, lanes), single),
             pltpu.VMEM((refs, devices, tall, lanes), single),
             pltpu.VMEM((devices, lanes, lanes), single),
             pltpu.VMEM((refs, lanes, extent), single),
             pltpu.VMEM((2, lanes, extent), single),
+            pltpu.SemaphoreType.DMA((2, devices)),
+            pltpu.SemaphoreType.DMA((2, devices)),
             pltpu.SemaphoreType.DMA((devices,)),
             pltpu.SemaphoreType.DMA((devices,)),
-            pltpu.SemaphoreType.DMA((devices,)),
-            pltpu.SemaphoreType.DMA((devices,)),
-            pltpu.SemaphoreType.DMA((refs, devices)),
-            pltpu.SemaphoreType.DMA((refs, devices)),
+            pltpu.SemaphoreType.DMA((refs, 2, half)),
+            pltpu.SemaphoreType.DMA((refs, 2, half)),
         ],
         compiler_params=pltpu.CompilerParams(
             collective_id=0, has_side_effects=True, vmem_limit_bytes=60 * 2**20
@@ -572,7 +629,7 @@
         and velocity.shape[0] == 1
         and wavefield.shape[2] == lanes
         and wavefield.shape[3] == devices * lanes
-        and devices in (2, 4, 8, 16)
+        and devices in (4, 8, 16)
     )
     if fits:
         return migrate(devices, wavefield, frequencies, velocity, bracket)

time: 230 us -> 182 us (0.79)
  Pallas kernels: 224 us -> 176 us
    pallas_call x1, Pallas kernels: 224 us -> 176 us  [migrate(): pl.pallas_call(lambda *args: migrate_kernel(devices, *args), out_shape=(j...]
where the time goes in v1:
time: 182 us; the launch traced here: 181 us
  Pallas kernels  176 us (97%)
  local copies, waits for them, and re-layouts  4.2 us (2%)
    pallas_call x1, Pallas kernels, migrate(): pl.pallas_call(lambda *args: migrate_kernel(devices, *args), out_shape=(j...  176 us
    unnamed x4, local copies, waits for them, and re-layouts  4.2 us

profile of v1, /device:TPU:29, one launch (start us, length us, event | category | flops | bytes accessed | tf_op | source)
XLA Modules:
  0.0 181.5 jit_solution(2974210181252829803)
XLA Ops:
  1.3 176.0 %shard_map.95 = (f32[1,2,128,2048]{3,2,1,0:T(8,128)}, f32[1,128,2048]{2,1,0:T(8,128)}) custom-call(f32[1,2,128,2048]{3,2,1,0:T(8,128)} %args_0_.4, f32[1]{0:T(128)S(6)} %copy.12.args_1_, f32[1,128,2048]{2,1,0:T(8,128)} %args_2_.4, s32[1,128,2048]{2,1,0:T(8,128)} %args_3_.4, bf16[16,256,256]{2,1,0:T(8,128)(2,1)} %constant.8.clone.args_4_, ...), custom_call_target="tpu_custom_call" | custom-call | tf_op jit(solution)/shard_map/pallas_call | solution.py:593
  177.3 0.0 copy-start
  177.3 3.2 %copy.13 = f32[1,2,128,2048]{3,2,1,0:T(8,128)} copy(f32[1,2,128,2048]{3,2,1,0:T(8,128)} %get-tuple-element.4) | data formatting | bytes 4194304
  180.5 0.0 copy-done
  180.5 1.0 copy.14
Async XLA Ops:
  177.3 3.2 %copy-start = (f32[1,128,2048]{2,1,0:T(8,128)S(1)}, f32[1,128,2048]{2,1,0:T(8,128)}, u32[]{:S(2)}) copy-start(f32[1,128,2048]{2,1,0:T(8,128)} %get-tuple-element.5) | copy-start | bytes 3145732

commit v2 on v1

--- a/solution.py
+++ b/solution.py
@@ -333,7 +333,7 @@
     wave_ref, freq_ref, vel_ref, bracket_ref, ah_ref, al_ref, th_ref, tl_ref,
     out_ref, image_ref,
     lines, sends, spec, factors, mixed, parts, waves, speed_recv, coef, turn,
-    send_f, recv_f, send_v, recv_v, send_p, recv_p,
+    send_f, recv_f, send_v, recv_v, send_p, recv_p, send_w, recv_w,
 ):
     me = lax.axis_index("slab")
     refs = len(ref_speeds)
@@ -353,10 +353,21 @@
             device_id={"slab": target}, device_id_type=pl.DeviceIdType.MESH,
         )
 
+    shot = lax.axis_index("shot")
+    own = pl.ds(pl.multiple_of(shot * (lanes // 2), lanes // 2), lanes // 2)
+    partner = {"shot": 1 - shot, "slab": me}
+
+    def speed_swap():
+        return pltpu.make_async_remote_copy(
+            src_ref=speed_recv.at[:, own], dst_ref=speed_recv.at[:, own],
+            send_sem=send_w, recv_sem=recv_w,
+            device_id=partner, device_id_type=pl.DeviceIdType.MESH,
+        )
+
     def speed_copy(target, block):
         return pltpu.make_async_remote_copy(
-            src_ref=vel_ref.at[0, :, pl.ds(pl.multiple_of(target * lanes, lanes), lanes)],
-            dst_ref=speed_recv.at[block],
+            src_ref=vel_ref.at[0, own, pl.ds(pl.multiple_of(target * lanes, lanes), lanes)],
+            dst_ref=speed_recv.at[block, own],
             send_sem=send_v.at[target], recv_sem=recv_v.at[block],
             device_id={"slab": target}, device_id_type=pl.DeviceIdType.MESH,
         )
@@ -387,6 +398,8 @@
         pl.semaphore_signal(
             barrier, inc=1, device_id={"slab": peer(step)}, device_id_type=pl.DeviceIdType.MESH
         )
+
+    pl.semaphore_signal(barrier, inc=1, device_id=partner, device_id_type=pl.DeviceIdType.MESH)
 
     @pl.loop(0, steps)
     def _(i):
@@ -402,7 +415,7 @@
             lines[k, rows, :lanes] = re
             lines[k, rows, lanes:] = im
 
-    pl.semaphore_wait(barrier, devices - 1)
+    pl.semaphore_wait(barrier, devices)
 
     for e in range(2):
 
@@ -420,10 +433,6 @@
                 forward_copy(e, base + k, me).start()
 
         spec[e, me] = sends[e * half + place]
-
-    @pl.loop(1, devices)
-    def _(step):
-        speed_copy(peer(step), me).start()
 
     angular = freq_ref[0]
     unit = 2.0 * math.pi / extent
@@ -478,6 +487,12 @@
             def _():
                 forward_copy(e, base + k, base + k).wait_recv()
 
+        if e == 1:
+
+            @pl.loop(1, devices)
+            def _(step):
+                speed_copy(peer(step), me).start()
+
         across(spec.at[e], spec.at[e], lambda values: butterflies(values, -1.0))
 
         for j in range(refs):
@@ -499,12 +514,34 @@
 
             waves[j, e * half + place] = parts[j, e, place]
 
-    speed_recv[me] = vel_ref[0, :, pl.ds(pl.multiple_of(me * lanes, lanes), lanes)]
+    def receive(j, e):
+        @pl.loop(0, half)
+        def _(step):
+            block = near_origin(step)
+            k = e * half + block
+
+            @pl.when(step > 0)
+            def _():
+                part_copy(j, e, block, block).wait_recv()
+
+            row = jnp.concatenate([waves[j, k, :lanes, :], waves[j, k, lanes:, :]], axis=1)
+            got = dot_right(row, th_ref[k], tl_ref[k])
+            waves[j, k, :lanes, :] = got[:, :lanes]
+            waves[j, k, lanes:, :] = got[:, lanes:]
+
+    speed_recv[me, own] = vel_ref[0, own, pl.ds(pl.multiple_of(me * lanes, lanes), lanes)]
 
     @pl.loop(1, devices)
     def _(step):
         k = origin(step)
         speed_copy(k, k).wait_recv()
+
+    speed_swap().start()
+
+    for j in range(refs):
+        receive(j, 0)
+
+    speed_swap().wait_recv()
 
     for a in range(devices):
         cols = slice(a * lanes, (a + 1) * lanes)
@@ -523,24 +560,6 @@
         u = angle * angle
         turn[0, :, cols] = horner([1.0, -1 / 2, 1 / 24, -1 / 720, 1 / 40320], u)
         turn[1, :, cols] = angle * horner([1.0, -1 / 6, 1 / 120, -1 / 5040], u)
-
-    def receive(j, e):
-        @pl.loop(0, half)
-        def _(step):
-            block = near_origin(step)
-            k = e * half + block
-
-            @pl.when(step > 0)
-            def _():
-                part_copy(j, e, block, block).wait_recv()
-
-            row = jnp.concatenate([waves[j, k, :lanes, :], waves[j, k, lanes:, :]], axis=1)
-            got = dot_right(row, th_ref[k], tl_ref[k])
-            waves[j, k, :lanes, :] = got[:, :lanes]
-            waves[j, k, lanes:, :] = got[:, lanes:]
-
-    for j in range(refs):
-        receive(j, 0)
 
     for j in range(refs):
         receive(j, 1)
@@ -563,6 +582,8 @@
                     image_ref[0, top, cols] = re
                 out_ref[0, 0, top, cols] = re
                 out_ref[0, 1, top, cols] = im
+
+    speed_swap().wait_send()
 
     @pl.loop(1, devices)
     def _(step):
@@ -615,6 +636,8 @@
             pltpu.SemaphoreType.DMA((devices,)),
             pltpu.SemaphoreType.DMA((refs, 2, half)),
             pltpu.SemaphoreType.DMA((refs, 2, half)),
+            pltpu.SemaphoreType.DMA,
+            pltpu.SemaphoreType.DMA,
         ],
         compiler_params=pltpu.CompilerParams(
             collective_id=0, has_side_effects=True, vmem_limit_bytes=60 * 2**20
@@ -630,6 +653,7 @@
         and wavefield.shape[2] == lanes
         and wavefield.shape[3] == devices * lanes
         and devices in (4, 8, 16)
+        and lax.axis_size("shot") == 2
     )
     if fits:
         return migrate(devices, wavefield, frequencies, velocity, bracket)

time: 182 us -> 180 us (0.989)
  Pallas kernels: 176 us -> 173 us
    pallas_call x1, Pallas kernels: 176 us -> 173 us  [migrate(): pl.pallas_call(lambda *args: migrate_kernel(devices, *args), out_shape=(j...]
where the time goes in v2:
time: 180 us; the launch traced here: 179 us
  Pallas kernels  173 us (96%)
  local copies, waits for them, and re-layouts  4.2 us (2%)
    pallas_call x1, Pallas kernels, migrate(): pl.pallas_call(lambda *args: migrate_kernel(devices, *args), out_shape=(j...  173 us
    unnamed x4, local copies, waits for them, and re-layouts  4.2 us

profile of v2, /device:TPU:29, one launch (start us, length us, event | category | flops | bytes accessed | tf_op | source)
XLA Modules:
  0.0 178.6 jit_solution(2174037525916930690)
XLA Ops:
  1.3 173.1 %shard_map.95 = (f32[1,2,128,2048]{3,2,1,0:T(8,128)}, f32[1,128,2048]{2,1,0:T(8,128)}) custom-call(f32[1,2,128,2048]{3,2,1,0:T(8,128)} %args_0_.4, f32[1]{0:T(128)S(6)} %copy.12.args_1_, f32[1,128,2048]{2,1,0:T(8,128)} %args_2_.4, s32[1,128,2048]{2,1,0:T(8,128)} %args_3_.4, bf16[16,256,256]{2,1,0:T(8,128)(2,1)} %constant.8.clone.args_4_, ...), custom_call_target="tpu_custom_call" | custom-call | tf_op jit(solution)/shard_map/pallas_call | solution.py:614
  174.4 0.0 copy-start
  174.4 3.2 %copy.13 = f32[1,2,128,2048]{3,2,1,0:T(8,128)} copy(f32[1,2,128,2048]{3,2,1,0:T(8,128)} %get-tuple-element.4) | data formatting | bytes 4194304
  177.6 0.0 copy-done
  177.6 1.0 copy.14
Async XLA Ops:
  174.4 3.2 %copy-start = (f32[1,128,2048]{2,1,0:T(8,128)S(1)}, f32[1,128,2048]{2,1,0:T(8,128)}, u32[]{:S(2)}) copy-start(f32[1,128,2048]{2,1,0:T(8,128)} %get-tuple-element.5) | copy-start | bytes 3145732

commit v3 on v2

--- a/solution.py
+++ b/solution.py
@@ -331,7 +331,7 @@
 def migrate_kernel(
     devices,
     wave_ref, freq_ref, vel_ref, bracket_ref, ah_ref, al_ref, th_ref, tl_ref,
-    out_ref, image_ref,
+    real_ref, imag_ref,
     lines, sends, spec, factors, mixed, parts, waves, speed_recv, coef, turn,
     send_f, recv_f, send_v, recv_v, send_p, recv_p, send_w, recv_w,
 ):
@@ -574,14 +574,13 @@
                 weight = coef[j, top, cols]
                 re, im = re * weight, im * weight
                 if j > 0:
-                    re = re + out_ref[0, 0, top, cols]
-                    im = im + out_ref[0, 1, top, cols]
+                    re = re + real_ref[0, top, cols]
+                    im = im + imag_ref[0, top, cols]
                 if j == refs - 1:
                     c, s = turn[0, top, cols], turn[1, top, cols]
                     re, im = re * c - im * s, re * s + im * c
-                    image_ref[0, top, cols] = re
-                out_ref[0, 0, top, cols] = re
-                out_ref[0, 1, top, cols] = im
+                real_ref[0, top, cols] = re
+                imag_ref[0, top, cols] = im
 
     speed_swap().wait_send()
 
@@ -611,10 +610,10 @@
     half = devices // 2
     tall = 2 * lanes
     single = jnp.float32
-    return pl.pallas_call(
+    real, imag = pl.pallas_call(
         lambda *args: migrate_kernel(devices, *args),
         out_shape=(
-            jax.ShapeDtypeStruct((1, 2, lanes, extent), single),
+            jax.ShapeDtypeStruct((1, lanes, extent), single),
             jax.ShapeDtypeStruct((1, lanes, extent), single),
         ),
         in_specs=[vmem, pl.BlockSpec(memory_space=pltpu.SMEM)] + [vmem] * 6,
@@ -643,6 +642,7 @@
             collective_id=0, has_side_effects=True, vmem_limit_bytes=60 * 2**20
         ),
     )(wavefield, frequencies, velocity, bracket, *tables)
+    return jnp.stack((real, imag), axis=1), real
 
 
 def on_device(wavefield, frequencies, velocity, bracket):

time: 180 us -> 179 us (level)
  local copies, waits for them, and re-layouts: 4.2 us -> 0.97 us
  other arithmetic: 0 us -> 3.17 us
    unnamed x4 -> x3, local copies, waits for them, and re-layouts: 4.2 us -> 0.97 us
    another operation x0 -> x1, other arithmetic: none -> 3.17 us  [migrate(): return (jnp.stack((real, imag), axis=1), real)]
where the time goes in v3:
time: 179 us; the launch traced here: 178 us
  Pallas kernels  173 us (97%)
  other arithmetic  3.17 us (2%)
    pallas_call x1, Pallas kernels, migrate(): pl.pallas_call(lambda *args: migrate_kernel(devices, *args), out_shape=(j...  173 us

profile of v3, /device:TPU:29, one launch (start us, length us, event | category | flops | bytes accessed | tf_op | source)
XLA Modules:
  0.0 178.2 jit_solution(1365413164148839894)
XLA Ops:
  1.3 172.8 %shard_map.95 = (f32[1,128,2048]{2,1,0:T(8,128)}, f32[1,128,2048]{2,1,0:T(8,128)}) custom-call(f32[1,2,128,2048]{3,2,1,0:T(8,128)} %args_0_.4, f32[1]{0:T(128)S(6)} %copy.11.args_1_, f32[1,128,2048]{2,1,0:T(8,128)} %args_2_.4, s32[1,128,2048]{2,1,0:T(8,128)} %args_3_.4, bf16[16,256,256]{2,1,0:T(8,128)(2,1)} %constant.8.clone.args_4_, ...), custom_call_target="tpu_custom_call" | custom-call | tf_op jit(solution)/shard_map/pallas_call | solution.py:613
  174.1 0.0 copy-start
  174.1 3.2 %pad_maximum_fusion = f32[1,2,128,2048]{3,2,1,0:T(8,128)} fusion(f32[1,1,128,2048]{3,2,1,0:T(8,128)} %bitcast.3, f32[1,1,128,2048]{3,2,1,0:T(8,128)} %bitcast.2), kind=kLoop, calls=%fused_computation | loop fusion | flops 524288 | bytes 4194304 | tf_op jit(solution)/shard_map/stack | solution.py:645
  177.2 0.0 copy-done
  177.2 1.0 copy.12
Async XLA Ops:
  174.1 3.2 %copy-start = (f32[1,128,2048]{2,1,0:T(8,128)S(1)}, f32[1,128,2048]{2,1,0:T(8,128)}, u32[]{:S(2)}) copy-start(f32[1,128,2048]{2,1,0:T(8,128)} %get-tuple-element.9) | copy-start | bytes 3145732
